TPU v7x, 32 devices: a whole 2x2x4 slice. The times are simulated.
32 devices in a mesh: row: 16 (over z, y, core), col: 2 (over x).
Axes of the slice: x: 2, y: 2, z: 4, core: 2. Of those that a mesh axis runs over, the one named last changes fastest.
Arguments:
- features: bfloat16 [12288, 512], P(('row', 'col')), may hold values from -6 to 6
- weight: bfloat16 [512, 512], replicated, may hold values from -0.25 to 0.25
- tile_values: bfloat16 [16, 2, 8, 128, 128], P('row', 'col'), may hold values from -0.3125 to 0.3125
- tile_rows: int32 [16, 2, 8], P('row', 'col'), may hold values from 0 to 5, as said below
- tile_cols: int32 [16, 2, 8], P('row', 'col'), may hold values from 0 to 47, as said below
- tile_count: int32 [16, 2], P('row', 'col'), may hold values from 1 to 8, as said below
- cotangent: bfloat16 [12288, 512], P(('row', 'col')), may hold values from -6 to 6
Outputs:
- activated: bfloat16 [12288, 512], P(('row', 'col'))
- grad_features: bfloat16 [12288, 512], P(('row', 'col'))
- grad_weight: float32 [512, 512], replicated
Inputs may be any that keep to these rules, and one draw needn't show every extreme that they name: `tile_rows`: within one block the live and dead slots name distinct tiles. `tile_cols`: within one block the live and dead slots name distinct tiles. `tile_count`: some block has all 8 slots live.
All inputs are finite; a program needn't handle non-finite values.
Results may differ from a plain program's by a relative error of at most 0.012.
Values may be sent and summed in bfloat16 or wider, within the bound.
A program may use at most 128 MiB of HBM per device.

v0:
```python
import jax
import jax.numpy as jnp
from jax import lax
from jax.sharding import PartitionSpec as P


def gelu_tanh(field):
    return jax.nn.gelu(field, approximate=True)


def per_device(features, weight, tile_values, tile_rows, tile_cols, tile_count, cotangent):
    rows_dev = features.shape[0]
    feat_width = features.shape[1]
    slot_total = tile_values.shape[2]
    tile_size = tile_values.shape[3]
    n_row = lax.axis_size("row")
    n_col = lax.axis_size("col")
    values = tile_values[0, 0]
    row_index = tile_rows[0, 0]
    col_index = tile_cols[0, 0]
    live_count = tile_count[0, 0]
    slot_block = min(8, slot_total)
    turns = (live_count + slot_block - 1) // slot_block
    row_tiles = rows_dev * n_col // tile_size
    col_tiles = rows_dev * n_row // tile_size

    def aggregate(source, source_index, target_index, target_tiles, transposed):
        source_tiles = source.reshape(-1, tile_size, feat_width)

        def add_block(step_index, totals):
            first_slot = step_index * slot_block
            block_values = lax.dynamic_slice_in_dim(values, first_slot, slot_block, 0)
            sources = lax.dynamic_slice_in_dim(source_index, first_slot, slot_block, 0)
            targets = lax.dynamic_slice_in_dim(target_index, first_slot, slot_block, 0)
            picked = source_tiles[sources]
            if transposed:
                products = jnp.einsum(
                    "kij,kif->kjf", block_values, picked, preferred_element_type=jnp.float32
                )
            else:
                products = jnp.einsum(
                    "kij,kjf->kif", block_values, picked, preferred_element_type=jnp.float32
                )
            active = first_slot + jnp.arange(slot_block) < live_count
            onehot = (
                (targets[:, None] == jnp.arange(target_tiles)[None, :]) & active[:, None]
            ).astype(jnp.float32)
            return totals + jnp.einsum(
                "kg,kif->gif", onehot, products, precision=lax.Precision.HIGHEST
            )

        totals = lax.fori_loop(
            0, turns, add_block, jnp.zeros((target_tiles, tile_size, feat_width), jnp.float32)
        )
        return totals.reshape(target_tiles * tile_size, feat_width)

    hidden = jnp.dot(features, weight, preferred_element_type=jnp.float32).astype(jnp.bfloat16)
    column_block = lax.all_gather(hidden, "row", axis=0, tiled=True)
    partial_value = aggregate(column_block, col_index, row_index, row_tiles, False)
    summed = lax.psum_scatter(
        partial_value.astype(jnp.bfloat16), "col", scatter_dimension=0, tiled=True
    ).astype(jnp.float32)
    activated = gelu_tanh(summed).astype(jnp.bfloat16)
    _, pullback = jax.vjp(gelu_tanh, summed)
    slope = pullback(cotangent.astype(jnp.float32))[0].astype(jnp.bfloat16)
    slope_block = lax.all_gather(slope, "col", axis=0, tiled=True)
    back_terms = aggregate(slope_block, row_index, col_index, col_tiles, True)
    grad_hidden = lax.psum_scatter(
        back_terms.astype(jnp.bfloat16), "row", scatter_dimension=0, tiled=True
    )
    grad_features = jnp.dot(grad_hidden, weight.T, preferred_element_type=jnp.float32).astype(
        jnp.bfloat16
    )
    local_weight = jnp.dot(features.T, grad_hidden, preferred_element_type=jnp.float32)
    node_total = rows_dev * n_row * n_col
    grad_weight = lax.psum(local_weight, ("row", "col")) * (1.0 / jnp.sqrt(jnp.float32(node_total)))
    return (activated, grad_features, grad_weight)


def solution(mesh):
    in_specs = (
        P(("row", "col"), None),
        P(),
        P("row", "col", None, None, None),
        P("row", "col", None),
        P("row", "col", None),
        P("row", "col"),
        P(("row", "col"), None),
    )
    out_specs = (P(("row", "col"), None), P(("row", "col"), None), P())
    return jax.shard_map(
        per_device, mesh=mesh, in_specs=in_specs, out_specs=out_specs, check_vma=False
    )
```

profile of v0, /device:TPU:0, one launch (start us, length us, event | category | flops | bytes accessed | tf_op | source)
XLA Modules:
  0.0 386.5 jit_solution(12004601706371520676)
XLA Ops:
  7.2 0.0 copy-start
  7.2 0.0 copy-start.1
  7.2 0.0 all-gather.2.cloned.1.call-start
  7.2 1.0 copy-done
  8.2 2.1 convolution_convert_fusion.1
  10.3 0.0 all-gather.2.cloned.1.call-update
  10.3 0.0 reduce-scatter.3.cloned.1.call-start
  11.1 0.7 fusion.28
  11.7 63.7 %all-gather.2.cloned.1.call-done = bf16[6144,512]{1,0:T(8,128)(2,1)} async-done(((bf16[384,512]{1,0:T(8,128)(2,1)}), bf16[6144,512]{1,0:T(8,128)(2,1)}) %all-gather.2.cloned.1.call-update) | async-done | bytes 6291472 | tf_op jit(solution)/shard_map/all_gather | solution.py:58
  75.5 4.4 %gather_fusion.1 = bf16[8,128,512]{2,1,0:T(8,128)(2,1)} fusion(bf16[48,128,512]{2,1,0:T(8,128)(2,1)} %bitcast.64, s32[1024]{0:T(1024)S(1)} %pad_clamp_fusion.1), kind=kCustom, calls=%fused_computation.1 | custom fusion | bytes 2097184 | tf_op jit(solution)/shard_map/while/body/gather | solution.py:35
  79.8 0.0 copy-done.1
  79.8 1.7 fusion.29
  81.6 2.1 copy.14
  83.6 0.0 copy-start.6
  83.6 0.2 broadcast_in_dim.4
  83.9 0.4 copy-done.6
  84.3 4.3 %while.22 = (s32[]{:T(128)}, f32[6,128,512]{2,0,1:T(8,128)S(1)}, s32[]{:T(128)}, s32[8]{0:T(128)S(1)}, s32[]{:T(128)}, /*index=5*/f32[8,512,128]{1,0,2:T(8,128)}, s32[]{:T(128)}, s32[]{:T(128)}) while((s32[]{:T(128)}, f32[6,128,512]{2,0,1:T(8,128)S(1)}, s32[]{:T(128)}, s32[8]{0:T(128)S(1)}, s32[]{:T(128)}, ...), condition=%wide.region_1.2_spmd, body=%wide.region_0.1_spmd.sunk | while | flops 38142064 | bytes 5243033 | solution.py:52
  84.3 0.7 add_compare_fusion.4
  84.9 3.6 fusion.52
  88.6 0.1 convert_element_type.33
  88.7 0.0 copy-start.4
  88.7 1.1 copy.15
  89.8 0.0 reduce-scatter.3.cloned.1.call-update
  89.9 0.0 reduce-scatter.5.cloned.1.call-start
  89.9 16.1 %reduce-scatter.3.cloned.1.call-done = bf16[384,512]{1,0:T(8,128)(2,1)} async-done(((bf16[768,512]{1,0:T(8,128)(2,1)}), bf16[384,512]{1,0:T(8,128)(2,1)}) %reduce-scatter.3.cloned.1.call-update) | async-done | bytes 393232 | tf_op jit(solution)/shard_map/reduce_scatter | solution.py:60
  106.0 0.0 copy-done.4
  106.0 2.4 fusion.20
  108.4 11.5 %all_gather.7 = bf16[768,512]{1,0:T(8,128)(2,1)S(1)} all-gather(bf16[384,512]{1,0:T(8,128)(2,1)S(1)} %get-tuple-element.186), channel_id=1, replica_groups=mesh['row'=16,'col'=2] {'col'}, dimensions={0}, use_global_device_ids=true | all-gather | bytes 1179648 | tf_op jit(solution)/shard_map/all_gather | solution.py:66
  119.9 0.0 copy-start.5
  119.9 6.1 %broadcast_in_dim.5 = f32[48,128,512]{2,0,1:T(8,128)} broadcast(f32[]{:T(128)} %constant.50.clone.1), dimensions={} | broadcast | bytes 12582916 | tf_op jit(solution)/shard_map/broadcast_in_dim | solution.py:53
  126.1 0.0 copy-done.5
  126.1 17.5 %while.23 = (s32[]{:T(128)}, f32[48,128,512]{2,0,1:T(8,128)}, s32[]{:T(128)}, s32[8]{0:T(128)S(1)}, s32[]{:T(128)}, /*index=5*/s32[8]{0:T(128)S(1)}, bf16[6,128,...) while((s32[]{:T(128)}, f32[48,128,512]{2,0,1:T(8,128)}, s32[]{:T(128)}, ...), condition=%wide.region_4.5_spmd, body=%wide.region_3.4_spmd.sunk | while | flops 439355200 | bytes 36966696 | solution.py:52
  126.1 0.7 add_compare_fusion.5
  126.7 1.6 gather_fusion
  128.3 1.8 fusion.58
  130.1 2.0 copy.23
  132.1 11.4 %convolution_add_fusion.2 = f32[48,128,512]{2,0,1:T(8,128)} fusion(f32[48,128,512]{2,0,1:T(8,128)} %get-tuple-element.311, f32[8,512,128]{1,0,2:T(8,128)} %copy.23, s32[8]{0:T(128)S(1)} %get-tuple-element.323, pred[8]{0:T(512)(128)(4,1)S(1)} %add_compare_fusion.5), kind=kOutput, calls=%fused_computation.11.clone.1 | convolution fusion | flops 305136384 | bytes 27263016 | tf_op jit(solution)/shard_map/while/body/kg,kif->gif/dot_general | solution.py:48
  143.5 13.8 %copy.21 = bf16[48,128,512]{2,1,0:T(8,128)(2,1)} copy(f32[48,128,512]{2,0,1:T(8,128)} %get-tuple-element.139) | data formatting | bytes 18874368 | tf_op jit(solution)/shard_map/while | solution.py:52
  157.4 0.0 copy-start.2
  157.4 0.0 reduce-scatter.5.cloned.1.call-update
  157.4 0.0 all-reduce.2.cloned.1.call-start
  157.5 85.3 %reduce-scatter.5.cloned.1.call-done = bf16[384,512]{1,0:T(8,128)(2,1)} async-done(((bf16[6144,512]{1,0:T(8,128)(2,1)}), bf16[384,512]{1,0:T(8,128)(2,1)}) %reduce-scatter.5.cloned.1.call-update) | async-done | bytes 393232 | tf_op jit(solution)/shard_map/reduce_scatter | solution.py:68
  242.8 0.0 copy-done.2
  242.8 0.0 copy-start.3
  242.8 2.5 convolution_bitcast_fusion
  245.3 0.0 all-reduce.2.cloned.1.call-update
  245.3 0.0 copy-done.3
  245.3 1.2 convolution_convert_fusion
  246.4 130.9 %all-reduce.2.cloned.1.call-done = f32[512,512]{0,1:T(8,128)} async-done(((f32[512,512]{0,1:T(8,128)}), f32[512,512]{0,1:T(8,128)}) %all-reduce.2.cloned.1.call-update) | async-done | bytes 1048592 | tf_op jit(solution)/shard_map/psum | solution.py:76
  377.3 1.3 broadcast_multiply_fusion
  378.7 1.3 copy.17
  (3 shorter events, 0.0 us)
Async XLA Ops:
  7.2 1.0 copy-start
  7.2 72.7 %copy-start.1 = (bf16[1,1,8,128,128]{4,3,2,1,0:T(8,128)(2,1)S(1)}, bf16[1,1,8,128,128]{4,3,2,1,0:T(8,128)(2,1)}, u32[]{:S(2)}) copy-start(bf16[1,1,8,128,128]{4,3,2,1,0:T(8,128)(2,1)} %param.13) | copy-start | bytes 786436
  7.2 68.3 %all-gather.2.cloned.1.call-start = ((), (), s32[]{:S(2)}) async-start(), calls=%async_computation.2 | async-start | bytes 6684672 | tf_op jit(solution)/shard_map/all_gather | solution.py:58
  10.3 95.7 %reduce-scatter.3.cloned.1.call-start = ((), (), s32[]{:S(2)}) async-start(), calls=%async_computation.3 | async-start | bytes 1179648 | tf_op jit(solution)/shard_map/reduce_scatter | solution.py:60
  83.6 0.7 copy-start.6
  88.7 17.3 %copy-start.4 = (bf16[384,512]{1,0:T(8,128)(2,1)S(1)}, bf16[384,512]{1,0:T(8,128)(2,1)}, u32[]{:S(2)}) copy-start(bf16[384,512]{1,0:T(8,128)(2,1)} %param.17) | copy-start | bytes 1179652
  89.9 152.9 %reduce-scatter.5.cloned.1.call-start = ((), (), s32[]{:S(2)}) async-start(), calls=%async_computation.4 | async-start | bytes 6684672 | tf_op jit(solution)/shard_map/reduce_scatter | solution.py:68
  119.9 6.1 %copy-start.5 = (s32[1,1,8]{2,1,0:T(1,128)S(1)}, s32[1,1,8]{2,1,0:T(1,128)}, u32[]{:S(2)}) copy-start(s32[1,1,8]{2,1,0:T(1,128)} %param.15) | copy-start | bytes 100
  157.4 85.4 %copy-start.2 = (bf16[384,512]{1,0:T(8,128)(2,1)S(1)}, bf16[384,512]{1,0:T(8,128)(2,1)}, u32[]{:S(2)}) copy-start(bf16[384,512]{1,0:T(8,128)(2,1)} %param.11) | copy-start | bytes 1179652
  157.4 219.9 %all-reduce.2.cloned.1.call-start = ((), (), s32[]{:S(2)}) async-start(), calls=%async_computation.5 | async-start | bytes 2097152 | tf_op jit(solution)/shard_map/psum | solution.py:76
  242.8 2.5 copy-start.3
Sparse Core Ops, SparseCore 0:
  10.9 64.5 all-gather.1
  90.0 16.0 reduce-scatter.2
  157.5 85.1 reduce-scatter.4
  248.4 128.8 all-reduce.1
where the time goes:
time: 387 us; the launch traced here: 386 us
  waiting for transfers between devices  296 us (76%)
  local copies, waits for them, and re-layouts  34 us (9%)
  matrix products  24.3 us (6%)
  between operations  14.5 us (4%)
  blocking collectives  11.5 us (3%)
  other arithmetic  5.82 us (2%)
    psum x1, waiting for transfers between devices, per_device(): lax.psum(local_weight, ('row', 'col'))  131 us
    reduce_scatter x1, waiting for transfers between devices, per_device(): lax.psum_scatter(back_terms.astype(jnp.bfloat16), 'row', scatter_dimensio...  85.3 us
    all_gather x1, waiting for transfers between devices, per_device(): column_block = lax.all_gather(hidden, 'row', axis=0, tiled=True)  63.7 us
    reduce_scatter x1, waiting for transfers between devices, per_device(): lax.psum_scatter(partial_value.astype(jnp.bfloat16), 'col', scatter_dimen...  16.1 us
    while x2, local copies, waits for them, and re-layouts, aggregate(): lax.fori_loop(0, turns, add_block, jnp.zeros((target_tiles, tile_size, fe...  15.9 us
    dot_general x2, matrix products, add_block(): jnp.einsum('kg,kif->gif', onehot, products, precision=lax.Precision.HIGHEST)  15.1 us
    all_gather x1, blocking collectives, per_device(): slope_block = lax.all_gather(slope, 'col', axis=0, tiled=True)  11.5 us
  transfers between devices with their start and end apart: 4, of which 4 were waited for; matrix products, arithmetic and copies ran while one was open for 0% of the time, Pallas kernels for 0%

commit v1 on v0

v1 whole, which is shorter than its diff:
```python
import functools
import math

import jax
import jax.numpy as jnp
from jax import lax
from jax.experimental import pallas as pl
from jax.experimental.pallas import tpu as pltpu
from jax.sharding import PartitionSpec as P

MESH = pl.DeviceIdType.MESH
BF = jnp.bfloat16
F32 = jnp.float32
RIGHT, LEFT = 0, 1


def dot(a, b):
    return jnp.dot(a, b, preferred_element_type=F32)


def kernel(
    dims, feat, weight, vals, tile_rows, tile_cols, tile_count, cot, act_out, gf_out, gw_out,
    gath0, gath1, vt, lhs, picked, own_part, fsend, frecv, ax, slope_v, gblk0, gblk1, tmp, ring_in, sib_in,
    gwf, ga, ar, bs, br, gq, gd, atot,
    ag_s, ag_r, as_s, as_r, fx_s, fx_r, gx_s, gx_r, rs_s, rs_r, rb_s, rb_r,
    a_s, a_r, b_s, b_r, c_s, c_r, d_s, d_r,
):
    n_row, n_col, slots, block, tile, width, per_dev = dims
    chips = n_row // 2
    half = chips // 2
    cut = width // 2
    group = 2 * n_col
    gpart = width // group
    owners = min(chips, gpart // 16)
    prow = gpart // owners
    turns = slots // block
    rows_dev = per_dev * tile
    gath, gblk = (gath0, gath1), (gblk0, gblk1)

    row, col = lax.axis_index("row"), lax.axis_index("col")
    chip, core = row // 2, row % 2
    place = jnp.where(chip % 2 == 0, chip // 2, (2 * chips - 1 - chip) // 2)

    def row_at(position, which):
        position = lax.rem(position + 2 * chips, chips)
        there = jnp.where(position < half, 2 * position, 2 * chips - 1 - 2 * position)
        return there * 2 + which

    ring = ((row_at(place + 1, core), col), (row_at(place - 1, core), col))
    sibling = (chip * 2 + 1 - core, col)
    member = core * n_col + col

    def group_peer(j):
        other = lax.rem(member + j, group)
        return other, (chip * 2 + other // n_col, lax.rem(other, n_col))

    def chip_peer(j):
        other = lax.rem(chip + j, chips)
        return other, (other * 2 + core, col)

    def remote(src, dst, send, recv, device):
        return pltpu.make_async_remote_copy(
            src_ref=src, dst_ref=dst, send_sem=send, recv_sem=recv,
            device_id=device, device_id_type=MESH,
        )

    barrier = pltpu.get_barrier_semaphore()
    for j in range(1, chips):
        pl.semaphore_signal(barrier, inc=1, device_id=chip_peer(j)[1], device_id_type=MESH)
    for j in range(1, group):
        pl.semaphore_signal(barrier, inc=1, device_id=group_peer(j)[1], device_id_type=MESH)
    pl.semaphore_wait(barrier, chips - 1 + group - 1)

    def piece(h, which_row):
        return gath[h].at[pl.ds(which_row * per_dev, per_dev)]

    def columns(h):
        return slice(h * cut, (h + 1) * cut)

    sends = []

    def ag_ring(way, s, h):
        sign = -1 if way == RIGHT else 1
        whose = row_at(place + sign * s, core)
        src = feat.at[:, :, pl.ds(h * cut, cut)] if s == 0 else piece(h, whose)
        return remote(src, piece(h, whose), ag_s.at[way, s, h], ag_r.at[way, s, h], ring[way])

    def ag_sib(offset, h):
        whose = row_at(place + offset, core)
        src = feat.at[:, :, pl.ds(h * cut, cut)] if offset == 0 else piece(h, whose)
        k = offset % chips
        return remote(src, piece(h, whose), as_s.at[k, h], as_r.at[k, h], sibling)

    def used(way, s, h):
        return s < half - 1 or h == way

    for h in range(2):
        for way in (RIGHT, LEFT):
            if used(way, 0, h):
                copy = ag_ring(way, 0, h)
                copy.start()
                sends.append(copy)
    for h in range(2):
        copy = ag_sib(0, h)
        copy.start()
        sends.append(copy)
    for h in range(2):
        gath[h][pl.ds(row * per_dev, per_dev)] = feat[:, :, columns(h)]

    if slots <= 8:
        for k in range(slots):
            vt[k] = vals[k].T
    else:
        @pl.loop(0, slots)
        def _(k):
            vt[k] = vals[k].T

    for s in range(half):
        for h in range(2):
            for way in (RIGHT, LEFT):
                if used(way, s, h):
                    ag_ring(way, s, h).wait_recv()
                    if s + 1 < half and used(way, s + 1, h):
                        copy = ag_ring(way, s + 1, h)
                        copy.start()
                        sends.append(copy)
                    copy = ag_sib((-1 - s) if way == RIGHT else (1 + s), h)
                    copy.start()
                    sends.append(copy)

    live = tile_count[0]

    def fill(source, index, h, turn):
        for k in range(block):
            picked[h, k * tile:(k + 1) * tile, :] = source[h][index[turn * block + k]]

    def product(matrices, index, base, source, source_index, h):
        def one(turn):
            if turns > 1:
                fill(source, source_index, h, turn)
            for k in range(block):
                slot = turn * block + k
                value = matrices[slot]
                for t in range(per_dev):
                    keep = jnp.logical_and(index[slot] == base + t, slot < live)
                    lhs[t * tile:(t + 1) * tile, k * tile:(k + 1) * tile] = lax.select(
                        keep, value, jnp.zeros_like(value)
                    )
            return dot(lhs[...], picked[h])

        if turns == 1:
            return one(0)
        return lax.fori_loop(
            1, turns, lambda turn, total: total + one(turn), one(0)
        )

    def part_copy(h, j):
        to = lax.rem(col + j, n_col)
        return remote(fsend.at[h, j], frecv.at[h, j], fx_s.at[h, j], fx_r.at[h, j], (row, to))

    for h in range(2):
        for offset in range(chips):
            ag_sib(offset, h).wait_recv()
        if turns == 1:
            fill(gath, tile_cols, h, 0)
        for j in range(1, n_col):
            to = lax.rem(col + j, n_col)
            fsend[h, j] = product(vals, tile_rows, to * per_dev, gath, tile_cols, h).astype(BF)
            copy = part_copy(h, j)
            copy.start()
            sends.append(copy)
        own_part[h] = product(vals, tile_rows, col * per_dev, gath, tile_cols, h)

    for copy in sends:
        copy.wait_send()
    sends = []

    summed = None
    for h in range(2):
        for j in range(1, n_col):
            part_copy(h, j).wait_recv()
        total = own_part[h]
        for j in range(1, n_col):
            total = total + frecv[h, j].astype(F32)
        ax[:, columns(h)] = total.astype(BF)
        term = dot(ax[:, columns(h)], weight[columns(h), :])
        summed = term if summed is None else summed + term

    scale = math.sqrt(2.0 / math.pi)
    square = summed * summed
    tanh = jnp.tanh(scale * (summed + 0.044715 * (square * summed)))
    act_out[...] = (0.5 * summed * (1.0 + tanh)).astype(BF)
    steep = 0.5 * (1.0 + tanh) + (0.5 * summed) * (1.0 - tanh * tanh) * (
        scale * (1.0 + (3 * 0.044715) * square)
    )
    slope_v[...] = (cot[...].astype(F32) * steep).astype(BF)

    def slope_copy(h, j):
        to = lax.rem(col + j, n_col)
        mine = gblk[h].at[pl.ds(col * per_dev, per_dev)]
        return remote(mine, mine, gx_s.at[h, j], gx_r.at[h, j], (row, to))

    def from_copy(h, j):
        whose = lax.rem(col - j + n_col, n_col)
        theirs = gblk[h].at[pl.ds(whose * per_dev, per_dev)]
        return remote(theirs, theirs, gx_s.at[h, j], gx_r.at[h, j], (row, lax.rem(col + j, n_col)))

    for h in range(2):
        moved = lax.dot_general(
            slope_v[...], weight[columns(h), :], (((1,), (1,)), ((), ())),
            preferred_element_type=F32,
        ).astype(BF)
        gblk[h][pl.ds(col * per_dev, per_dev)] = moved.reshape(per_dev, tile, cut)
        for j in range(1, n_col):
            copy = slope_copy(h, j)
            copy.start()
            sends.append(copy)

    gwf[...] = lax.dot_general(
        ax[...], slope_v[...], (((0,), (0,)), ((), ())), preferred_element_type=F32
    ).reshape(group, gpart, width)
    ga[...] = gwf[...].astype(BF)

    def a_copy(j):
        other, device = group_peer(j)
        return remote(ga.at[other], ar.at[j], a_s.at[j], a_r.at[j], device)

    def b_copy(j):
        other, device = chip_peer(j)
        return other, remote(
            bs.at[lax.rem(other, owners)], br.at[j], b_s.at[j], b_r.at[j], device
        )

    def c_copy(j, whose):
        _, device = chip_peer(j)
        spot = gq.at[lax.rem(whose, owners)]
        return remote(spot, spot, c_s.at[j], c_r.at[j], device)

    def d_copy(j, whose):
        _, device = group_peer(j)
        return remote(gq, gd.at[whose], d_s.at[j], d_r.at[j], device)

    def when(condition, run):
        if owners == chips:
            run()
        else:
            pl.when(condition)(run)

    def stage_a():
        for j in range(1, group):
            copy = a_copy(j)
            copy.start()

    def stage_b():
        total = gwf[member]
        for j in range(1, group):
            a_copy(j).wait_recv()
            total = total + ar[j].astype(F32)
        atot[...] = total.reshape(owners, prow, width)
        bs[...] = atot[...].astype(BF)
        for j in range(1, chips):
            other, copy = b_copy(j)
            when(other < owners, copy.start)

    def stage_c():
        def reduce():
            total = atot[lax.rem(chip, owners)]
            for j in range(1, chips):
                b_copy(j)[1].wait_recv()
                total = total + br[j].astype(F32)
            node_total = rows_dev * n_row * n_col
            gq[lax.rem(chip, owners)] = (total * (1.0 / math.sqrt(node_total))).astype(BF)
            for j in range(1, chips):
                c_copy(j, chip).start()

        when(chip < owners, reduce)

    def stage_d():
        for j in range(1, chips):
            whose = lax.rem(chip - j + chips, chips)
            when(whose < owners, c_copy(j, whose).wait_recv)
        for j in range(1, group):
            d_copy(j, member).start()

    def finish():
        for j in range(1, group):
            d_copy(j, lax.rem(member - j + group, group)).wait_recv()
            whose = lax.rem(member - j + group, group)
            gw_out[whose] = gd[whose].reshape(gpart, width).astype(F32)
        gw_out[member] = gq[...].reshape(gpart, width).astype(F32)
        for j in range(1, group):
            a_copy(j).wait_send()
            d_copy(j, member).wait_send()
        for j in range(1, chips):
            other, copy = b_copy(j)
            when(other < owners, copy.wait_send)
            when(chip < owners, c_copy(j, chip).wait_send)

    stage_a()

    def term(offset, which, h):
        dest = row_at(place + offset, which)
        return product(vt, tile_cols, dest * per_dev, gblk, tile_rows, h)

    def rb_copy(offset, h):
        k = offset % chips
        return remote(
            piece(h, row_at(place + offset, 1 - core)), sib_in.at[k, h],
            rb_s.at[k, h], rb_r.at[k, h], sibling,
        )

    def rs_copy(way, s, h):
        offset = half - s if way == RIGHT else s - half
        return remote(
            piece(h, row_at(place + offset, core)), ring_in.at[way, s, h],
            rs_s.at[way, s, h], rs_r.at[way, s, h], ring[way],
        )

    def items(s):
        if s == 0:
            return [(RIGHT, 0), (LEFT, 1)]
        if s == half:
            return [(None, 0), (None, 1)]
        return [(RIGHT, 0), (LEFT, 0), (RIGHT, 1), (LEFT, 1)]

    def offset_of(way, s):
        if way is None:
            return 0
        return half - s if way == RIGHT else s - half

    def give(s, way, h):
        offset = offset_of(way, s)
        out = term(offset, 1 - core, h).astype(BF)
        gath[h][pl.ds(row_at(place + offset, 1 - core) * per_dev, per_dev)] = out.reshape(
            per_dev, tile, cut
        )
        copy = rb_copy(offset, h)
        copy.start()
        sends.append(copy)

    def arrive(h):
        for j in range(1, n_col):
            from_copy(h, j).wait_recv()
        if turns == 1:
            fill(gblk, tile_rows, h, 0)

    def came(way, s, h):
        return s > 0 or h == way

    for way, h in items(0):
        arrive(h)
        give(0, way, h)
        tmp[h] = term(offset_of(way, 0), core, h)
    for s in range(half + 1):
        now = items(s)
        if s > 0:
            for n, (way, h) in enumerate(now):
                tmp[n] = term(offset_of(way, s), core, h)
        for n, (way, h) in enumerate(now):
            offset = offset_of(way, s)
            total = tmp[n]
            rb_copy(offset, h).wait_recv()
            total = total + sib_in[offset % chips, h].astype(F32).reshape(rows_dev, cut)
            for source in ((RIGHT, LEFT) if way is None else (way,)):
                if s > 0 and came(source, s - 1, h):
                    rs_copy(source, s - 1, h).wait_recv()
                    total = total + ring_in[source, s - 1, h].astype(F32).reshape(rows_dev, cut)
            if way is None:
                gf_out[:, columns(h)] = total.astype(BF)
            else:
                gath[h][pl.ds(row_at(place + offset, core) * per_dev, per_dev)] = total.astype(
                    BF
                ).reshape(per_dev, tile, cut)
                copy = rs_copy(way, s, h)
                copy.start()
                sends.append(copy)
        if s < half:
            for way, h in items(s + 1):
                give(s + 1, way, h)
        if s == 0:
            stage_b()
        if s == min(1, half - 1):
            stage_c()
        if s == min(2, half - 1):
            stage_d()
    finish()
    for copy in sends:
        copy.wait_send()


def per_device(features, weight, tile_values, tile_rows, tile_cols, tile_count, cotangent):
    rows_dev, width = features.shape
    slots, tile = tile_values.shape[2], tile_values.shape[3]
    n_row, n_col = lax.axis_size("row"), lax.axis_size("col")
    per_dev = rows_dev // tile
    block = min(8, slots)
    chips = n_row // 2
    half = chips // 2
    cut = width // 2
    group = 2 * n_col
    gpart = width // group
    owners = min(chips, gpart // 16)
    prow = gpart // owners
    dims = (n_row, n_col, slots, block, tile, width, per_dev)
    dma = lambda *shape: pltpu.SemaphoreType.DMA(shape)
    vmem = pl.BlockSpec(memory_space=pltpu.VMEM)
    smem = pl.BlockSpec(memory_space=pltpu.SMEM)
    act, gf, gw = pl.pallas_call(
        functools.partial(kernel, dims),
        out_shape=(
            jax.ShapeDtypeStruct((rows_dev, width), BF),
            jax.ShapeDtypeStruct((rows_dev, width), BF),
            jax.ShapeDtypeStruct((group, gpart, width), F32),
        ),
        in_specs=[vmem, vmem, vmem, smem, smem, smem, vmem],
        out_specs=(vmem, vmem, vmem),
        scratch_shapes=[
            pltpu.VMEM((n_row * per_dev, tile, cut), BF),
            pltpu.VMEM((n_row * per_dev, tile, cut), BF),
            pltpu.VMEM((slots, tile, tile), BF),
            pltpu.VMEM((rows_dev, block * tile), BF),
            pltpu.VMEM((2, block * tile, cut), BF),
            pltpu.VMEM((2, rows_dev, cut), F32),
            pltpu.VMEM((2, n_col, rows_dev, cut), BF),
            pltpu.VMEM((2, n_col, rows_dev, cut), BF),
            pltpu.VMEM((rows_dev, width), BF),
            pltpu.VMEM((rows_dev, width), BF),
            pltpu.VMEM((n_col * per_dev, tile, cut), BF),
            pltpu.VMEM((n_col * per_dev, tile, cut), BF),
            pltpu.VMEM((4, rows_dev, cut), F32),
            pltpu.VMEM((2, half, 2, per_dev, tile, cut), BF),
            pltpu.VMEM((chips, 2, per_dev, tile, cut), BF),
            pltpu.VMEM((group, gpart, width), F32),
            pltpu.VMEM((group, gpart, width), BF),
            pltpu.VMEM((group, gpart, width), BF),
            pltpu.VMEM((owners, prow, width), BF),
            pltpu.VMEM((chips, prow, width), BF),
            pltpu.VMEM((owners, prow, width), BF),
            pltpu.VMEM((group, owners, prow, width), BF),
            pltpu.VMEM((owners, prow, width), F32),
            dma(2, half, 2), dma(2, half, 2), dma(chips, 2), dma(chips, 2),
            dma(2, n_col), dma(2, n_col), dma(2, n_col), dma(2, n_col),
            dma(2, half, 2), dma(2, half, 2), dma(chips, 2), dma(chips, 2),
            dma(group), dma(group), dma(chips), dma(chips),
            dma(chips), dma(chips), dma(group), dma(group),
        ],
        compiler_params=pltpu.CompilerParams(
            collective_id=0, has_side_effects=True, vmem_limit_bytes=58 * 1024 * 1024
        ),
        name="graph_layer",
    )(
        features.reshape(per_dev, tile, width),
        weight,
        tile_values[0, 0],
        tile_rows[0, 0],
        tile_cols[0, 0],
        tile_count[0],
        cotangent,
    )
    return act, gf, gw.reshape(width, width)


def solution(mesh):
    in_specs = (
        P(("row", "col"), None),
        P(),
        P("row", "col", None, None, None),
        P("row", "col", None),
        P("row", "col", None),
        P("row", "col"),
        P(("row", "col"), None),
    )
    out_specs = (P(("row", "col"), None), P(("row", "col"), None), P())
    return jax.shard_map(
        per_device, mesh=mesh, in_specs=in_specs, out_specs=out_specs, check_vma=False
    )
```

time: 387 us -> 109 us (0.28)
  waiting for transfers between devices: 296 us -> 0 us
  Pallas kernels: 0 us -> 103 us
  local copies, waits for them, and re-layouts: 34 us -> 4.59 us
  matrix products: 24.3 us -> 0 us
  between operations: 14.5 us -> 1.3 us
  blocking collectives: 11.5 us -> 0 us
  other arithmetic: 5.82 us -> 0 us
    psum x1 -> x0, waiting for transfers between devices: 131 us -> none  [per_device(): lax.psum(local_weight, ('row', 'col'))]
    pallas_call x0 -> x1, Pallas kernels: none -> 103 us  [per_device(): pl.pallas_call(functools.partial(kernel, dims), out_shape=(jax.ShapeDtype...]
    reduce_scatter x2 -> x0, waiting for transfers between devices: 101 us -> none  [the longest x1 85.3 us: per_device(): lax.psum_scatter(back_terms.astype(jnp.bfloat16), 'row', scatter_dimensio...]
    all_gather x1 -> x0, waiting for transfers between devices: 63.7 us -> none  [per_device(): column_block = lax.all_gather(hidden, 'row', axis=0, tiled=True)]
    dot_general x7 -> x0, matrix products: 24.3 us -> none  [the longest x2 15.1 us: add_block(): jnp.einsum('kg,kif->gif', onehot, products, precision=lax.Precision.HIGHEST)]
    while x2 -> x0, local copies, waits for them, and re-layouts: 15.9 us -> none  [aggregate(): lax.fori_loop(0, turns, add_block, jnp.zeros((target_tiles, tile_size, fe...]
    all_gather x1 -> x0, blocking collectives: 11.5 us -> none  [per_device(): slope_block = lax.all_gather(slope, 'col', axis=0, tiled=True)]
    broadcast_in_dim x2 -> x0, local copies, waits for them, and re-layouts: 6.38 us -> none  [aggregate(): jnp.zeros((target_tiles, tile_size, feat_width), jnp.float32)]
  transfers between devices with their start and end apart: 4 -> 0, of which waited for: 4 -> 0; matrix products, arithmetic and copies ran while one was open for 0% -> 0% of each run, Pallas kernels for 0% -> 0%
where the time goes in v1:
time: 109 us
  Pallas kernels  103 us (94%)
  local copies, waits for them, and re-layouts  4.59 us (4%)
  between operations  1.3 us (1%)
    pallas_call x1, Pallas kernels, per_device(): pl.pallas_call(functools.partial(kernel, dims), out_shape=(jax.ShapeDtype...  103 us
    unnamed x5, local copies, waits for them, and re-layouts  4.59 us

profile of v1, /device:TPU:0, one launch (start us, length us, event | category | flops | bytes accessed | tf_op | source)
XLA Modules:
  0.0 109.0 jit_solution(17898302736640850797)
XLA Ops:
  1.3 103.1 %graph_layer.1 = (bf16[384,512]{1,0:T(8,128)(2,1)}, bf16[384,512]{1,0:T(8,128)(2,1)}, f32[4,128,512]{2,1,0:T(8,128)}) custom-call(bf16[3,128,512]{2,1,0:T(8,128)(2,1)} %bitcast.8, bf16[512,512]{1,0:T(8,128)(2,1)} %weight.1, bf16[8,128,128]{2,1,0:T(8,128)(2,1)} %bitcast.9, s32[8]{0:T(128)} %bitcast.10, s32[8]{0:T(128)} %bitcast.11, s32[1]{0:T(128)} %bitcast.6.tile_count, ...), custom_call_target="tpu_custom_call" | custom-call | tf_op jit(solution)/shard_map/graph_layer/pallas_call | solution.py:408
  104.3 0.0 copy-start
  104.4 1.9 %copy.14 = bf16[384,512]{1,0:T(8,128)(2,1)} copy(bf16[384,512]{1,0:T(8,128)(2,1)} %get-tuple-element.12) | data formatting | bytes 786432
  106.2 1.8 %copy.15 = bf16[384,512]{1,0:T(8,128)(2,1)} copy(bf16[384,512]{1,0:T(8,128)(2,1)} %get-tuple-element.13) | data formatting | bytes 786432
  108.0 0.0 copy-done
  108.0 1.0 copy.16
Async XLA Ops:
  104.3 3.6 %copy-start = (f32[4,128,512]{2,1,0:T(8,128)S(1)}, f32[4,128,512]{2,1,0:T(8,128)}, u32[]{:S(2)}) copy-start(f32[4,128,512]{2,1,0:T(8,128)} %get-tuple-element.8) | copy-start | bytes 3145732

commit v2 on v1

--- a/solution.py
+++ b/solution.py
@@ -79,11 +79,12 @@
 
     sends = []
 
-    def ag_ring(way, s, h):
+    def ag_ring(way, s, h, t):
         sign = -1 if way == RIGHT else 1
         whose = row_at(place + sign * s, core)
-        src = feat.at[:, :, pl.ds(h * cut, cut)] if s == 0 else piece(h, whose)
-        return remote(src, piece(h, whose), ag_s.at[way, s, h], ag_r.at[way, s, h], ring[way])
+        dst = gath[h].at[whose * per_dev + t]
+        src = feat.at[t, :, pl.ds(h * cut, cut)] if s == 0 else dst
+        return remote(src, dst, ag_s.at[way, s, h, t], ag_r.at[way, s, h, t], ring[way])
 
     def ag_sib(offset, h):
         whose = row_at(place + offset, core)
@@ -94,12 +95,14 @@
     def used(way, s, h):
         return s < half - 1 or h == way
 
-    for h in range(2):
+    def ag_start(way, s, h, t):
+        copy = ag_ring(way, s, h, t)
+        copy.start()
+        sends.append(copy)
+
+    for t in range(per_dev):
         for way in (RIGHT, LEFT):
-            if used(way, 0, h):
-                copy = ag_ring(way, 0, h)
-                copy.start()
-                sends.append(copy)
+            ag_start(way, 0, 0, t)
     for h in range(2):
         copy = ag_sib(0, h)
         copy.start()
@@ -114,19 +117,6 @@
         @pl.loop(0, slots)
         def _(k):
             vt[k] = vals[k].T
-
-    for s in range(half):
-        for h in range(2):
-            for way in (RIGHT, LEFT):
-                if used(way, s, h):
-                    ag_ring(way, s, h).wait_recv()
-                    if s + 1 < half and used(way, s + 1, h):
-                        copy = ag_ring(way, s + 1, h)
-                        copy.start()
-                        sends.append(copy)
-                    copy = ag_sib((-1 - s) if way == RIGHT else (1 + s), h)
-                    copy.start()
-                    sends.append(copy)
 
     live = tile_count[0]
 
@@ -158,7 +148,7 @@
         to = lax.rem(col + j, n_col)
         return remote(fsend.at[h, j], frecv.at[h, j], fx_s.at[h, j], fx_r.at[h, j], (row, to))
 
-    for h in range(2):
+    def forward(h):
         for offset in range(chips):
             ag_sib(offset, h).wait_recv()
         if turns == 1:
@@ -171,6 +161,27 @@
             sends.append(copy)
         own_part[h] = product(vals, tile_rows, col * per_dev, gath, tile_cols, h)
 
+    for h in range(2):
+        for s in range(half):
+            for t in range(per_dev):
+                for way in (RIGHT, LEFT):
+                    if used(way, s, h):
+                        ag_ring(way, s, h, t).wait_recv()
+                        if s + 1 < half and used(way, s + 1, h):
+                            ag_start(way, s + 1, h, t)
+            for way in (RIGHT, LEFT):
+                if h == 0 and used(way, s, h) and not (s + 2 < half and used(way, s + 2, h)):
+                    if s + 1 < half and used(way, s + 1, h):
+                        for t in range(per_dev):
+                            ag_start(way, 0, 1, t)
+                if used(way, s, h):
+                    copy = ag_sib((-1 - s) if way == RIGHT else (1 + s), h)
+                    copy.start()
+                    sends.append(copy)
+            if h == 1 and s == 0:
+                forward(0)
+    forward(1)
+
     for copy in sends:
         copy.wait_send()
     sends = []
@@ -216,11 +227,6 @@
             copy.start()
             sends.append(copy)
 
-    gwf[...] = lax.dot_general(
-        ax[...], slope_v[...], (((0,), (0,)), ((), ())), preferred_element_type=F32
-    ).reshape(group, gpart, width)
-    ga[...] = gwf[...].astype(BF)
-
     def a_copy(j):
         other, device = group_peer(j)
         return remote(ga.at[other], ar.at[j], a_s.at[j], a_r.at[j], device)
@@ -247,6 +253,10 @@
             pl.when(condition)(run)
 
     def stage_a():
+        gwf[...] = lax.dot_general(
+            ax[...], slope_v[...], (((0,), (0,)), ((), ())), preferred_element_type=F32
+        ).reshape(group, gpart, width)
+        ga[...] = gwf[...].astype(BF)
         for j in range(1, group):
             copy = a_copy(j)
             copy.start()
@@ -286,8 +296,8 @@
         for j in range(1, group):
             d_copy(j, lax.rem(member - j + group, group)).wait_recv()
             whose = lax.rem(member - j + group, group)
-            gw_out[whose] = gd[whose].reshape(gpart, width).astype(F32)
-        gw_out[member] = gq[...].reshape(gpart, width).astype(F32)
+            gw_out[whose] = gd[whose].reshape(gpart, width)
+        gw_out[member] = gq[...].reshape(gpart, width)
         for j in range(1, group):
             a_copy(j).wait_send()
             d_copy(j, member).wait_send()
@@ -296,8 +306,6 @@
             when(other < owners, copy.wait_send)
             when(chip < owners, c_copy(j, chip).wait_send)
 
-    stage_a()
-
     def term(offset, which, h):
         dest = row_at(place + offset, which)
         return product(vt, tile_cols, dest * per_dev, gblk, tile_rows, h)
@@ -309,19 +317,17 @@
             rb_s.at[k, h], rb_r.at[k, h], sibling,
         )
 
-    def rs_copy(way, s, h):
+    def rs_copy(way, s, h, t):
         offset = half - s if way == RIGHT else s - half
         return remote(
-            piece(h, row_at(place + offset, core)), ring_in.at[way, s, h],
-            rs_s.at[way, s, h], rs_r.at[way, s, h], ring[way],
+            gath[h].at[row_at(place + offset, core) * per_dev + t], ring_in.at[way, s, h, t],
+            rs_s.at[way, s, h, t], rs_r.at[way, s, h, t], ring[way],
         )
 
-    def items(s):
+    def items(s, h):
         if s == 0:
-            return [(RIGHT, 0), (LEFT, 1)]
-        if s == half:
-            return [(None, 0), (None, 1)]
-        return [(RIGHT, 0), (LEFT, 0), (RIGHT, 1), (LEFT, 1)]
+            return [(RIGHT, LEFT)[h]]
+        return [None] if s == half else [RIGHT, LEFT]
 
     def offset_of(way, s):
         if way is None:
@@ -347,45 +353,54 @@
     def came(way, s, h):
         return s > 0 or h == way
 
-    for way, h in items(0):
-        arrive(h)
-        give(0, way, h)
-        tmp[h] = term(offset_of(way, 0), core, h)
-    for s in range(half + 1):
-        now = items(s)
-        if s > 0:
-            for n, (way, h) in enumerate(now):
-                tmp[n] = term(offset_of(way, s), core, h)
-        for n, (way, h) in enumerate(now):
+    order = [(0, 0), (1, 0), (0, 1)] + [(s, 0) for s in range(2, half)]
+    order += [(1, 1), (half, 0)] + [(s, 1) for s in range(2, half + 1)]
+    stages = {0: stage_a, 2: stage_b, 4: stage_c, 6: stage_d}
+
+    def give_all(n):
+        s, h = order[n]
+        if s == 0:
+            arrive(h)
+        for way in items(s, h):
+            give(s, way, h)
+
+    give_all(0)
+    for n, (s, h) in enumerate(order):
+        for m, way in enumerate(items(s, h)):
+            tmp[m] = term(offset_of(way, s), core, h)
+        for m, way in enumerate(items(s, h)):
             offset = offset_of(way, s)
-            total = tmp[n]
             rb_copy(offset, h).wait_recv()
-            total = total + sib_in[offset % chips, h].astype(F32).reshape(rows_dev, cut)
-            for source in ((RIGHT, LEFT) if way is None else (way,)):
-                if s > 0 and came(source, s - 1, h):
-                    rs_copy(source, s - 1, h).wait_recv()
-                    total = total + ring_in[source, s - 1, h].astype(F32).reshape(rows_dev, cut)
-            if way is None:
-                gf_out[:, columns(h)] = total.astype(BF)
-            else:
-                gath[h][pl.ds(row_at(place + offset, core) * per_dev, per_dev)] = total.astype(
-                    BF
-                ).reshape(per_dev, tile, cut)
-                copy = rs_copy(way, s, h)
-                copy.start()
-                sends.append(copy)
-        if s < half:
-            for way, h in items(s + 1):
-                give(s + 1, way, h)
-        if s == 0:
-            stage_b()
-        if s == min(1, half - 1):
-            stage_c()
-        if s == min(2, half - 1):
-            stage_d()
+            tmp[m] += sib_in[offset % chips, h].astype(F32).reshape(rows_dev, cut)
+        for t in range(per_dev):
+            rows = slice(t * tile, (t + 1) * tile)
+            for m, way in enumerate(items(s, h)):
+                total = tmp[m, rows]
+                for source in ((RIGHT, LEFT) if way is None else (way,)):
+                    if s > 0 and came(source, s - 1, h):
+                        rs_copy(source, s - 1, h, t).wait_recv()
+                        total = total + ring_in[source, s - 1, h, t].astype(F32)
+                if way is None:
+                    gf_out[rows, columns(h)] = total.astype(BF)
+                else:
+                    dest = row_at(place + offset_of(way, s), core)
+                    gath[h][dest * per_dev + t] = total.astype(BF)
+                    copy = rs_copy(way, s, h, t)
+                    copy.start()
+                    sends.append(copy)
+        if n + 1 < len(order):
+            give_all(n + 1)
+        if n in stages:
+            stages[n]()
     finish()
     for copy in sends:
         copy.wait_send()
+
+
+def write(act, gf, gw, act_out, gf_out, gw_out):
+    act_out[...] = act[...]
+    gf_out[...] = gf[...]
+    gw_out[...] = gw[...].astype(F32)
 
 
 def per_device(features, weight, tile_values, tile_rows, tile_cols, tile_count, cotangent):
@@ -410,7 +425,7 @@
         out_shape=(
             jax.ShapeDtypeStruct((rows_dev, width), BF),
             jax.ShapeDtypeStruct((rows_dev, width), BF),
-            jax.ShapeDtypeStruct((group, gpart, width), F32),
+            jax.ShapeDtypeStruct((group, gpart, width), BF),
         ),
         in_specs=[vmem, vmem, vmem, smem, smem, smem, vmem],
         out_specs=(vmem, vmem, vmem),
@@ -438,9 +453,9 @@
             pltpu.VMEM((owners, prow, width), BF),
             pltpu.VMEM((group, owners, prow, width), BF),
             pltpu.VMEM((owners, prow, width), F32),
-            dma(2, half, 2), dma(2, half, 2), dma(chips, 2), dma(chips, 2),
+            dma(2, half, 2, per_dev), dma(2, half, 2, per_dev), dma(chips, 2), dma(chips, 2),
             dma(2, n_col), dma(2, n_col), dma(2, n_col), dma(2, n_col),
-            dma(2, half, 2), dma(2, half, 2), dma(chips, 2), dma(chips, 2),
+            dma(2, half, 2, per_dev), dma(2, half, 2, per_dev), dma(chips, 2), dma(chips, 2),
             dma(group), dma(group), dma(chips), dma(chips),
             dma(chips), dma(chips), dma(group), dma(group),
         ],
@@ -457,7 +472,17 @@
         tile_count[0],
         cotangent,
     )
-    return act, gf, gw.reshape(width, width)
+    return pl.pallas_call(
+        write,
+        out_shape=(
+            jax.ShapeDtypeStruct((rows_dev, width), BF),
+            jax.ShapeDtypeStruct((rows_dev, width), BF),
+            jax.ShapeDtypeStruct((width, width), F32),
+        ),
+        in_specs=[vmem, vmem, vmem],
+        out_specs=(vmem, vmem, vmem),
+        name="write",
+    )(act, gf, gw.reshape(width, width))
 
 
 def solution(mesh):

time: 109 us -> 108 us (level)
  local copies, waits for them, and re-layouts: 4.59 us -> 0 us
  Pallas kernels: 103 us -> 106 us
    unnamed x5 -> x0, local copies, waits for them, and re-layouts: 4.59 us -> none
    pallas_call x0 -> x1, Pallas kernels: none -> 2.54 us  [per_device(): pl.pallas_call(write, out_shape=(jax.ShapeDtypeStruct((rows_dev, width),...]
where the time goes in v2:
time: 108 us; the launch traced here: 107 us
  Pallas kernels  106 us (98%)
  between operations  1.29 us (1%)
    pallas_call x1, Pallas kernels, per_device(): pl.pallas_call(functools.partial(kernel, dims), out_shape=(jax.ShapeDtype...  104 us
    pallas_call x1, Pallas kernels, per_device(): pl.pallas_call(write, out_shape=(jax.ShapeDtypeStruct((rows_dev, width),...  2.54 us

profile of v2, /device:TPU:0, one launch (start us, length us, event | category | flops | bytes accessed | tf_op | source)
XLA Modules:
  0.0 107.5 jit_solution(1325680058527744256)
XLA Ops:
  1.3 103.7 %graph_layer.1 = (bf16[384,512]{1,0:T(8,128)(2,1)}, bf16[384,512]{1,0:T(8,128)(2,1)}, bf16[4,128,512]{2,1,0:T(8,128)(2,1)}) custom-call(bf16[3,128,512]{2,1,0:T(8,128)(2,1)} %bitcast.8, bf16[512,512]{1,0:T(8,128)(2,1)} %weight.1, bf16[8,128,128]{2,1,0:T(8,128)(2,1)} %bitcast.9, s32[8]{0:T(128)} %bitcast.10, s32[8]{0:T(128)} %bitcast.11, ...), custom_call_target="tpu_custom_call" | custom-call | tf_op jit(solution)/shard_map/graph_layer/pallas_call | solution.py:423
  105.0 2.5 %write.1 = (bf16[384,512]{1,0:T(8,128)(2,1)}, bf16[384,512]{1,0:T(8,128)(2,1)}, f32[512,512]{1,0:T(8,128)}) custom-call(bf16[384,512]{1,0:T(8,128)(2,1)} %get-tuple-element.6.act, bf16[384,512]{1,0:T(8,128)(2,1)} %get-tuple-element.7.gf, bf16[512,512]{1,0:T(8,128)(2,1)} %bitcast.7), custom_call_target="tpu_custom_call" | custom-call | tf_op jit(solution)/shard_map/write/pallas_call | solution.py:475

commit v3 on v2

--- a/solution.py
+++ b/solution.py
@@ -353,8 +353,7 @@
     def came(way, s, h):
         return s > 0 or h == way
 
-    order = [(0, 0), (1, 0), (0, 1)] + [(s, 0) for s in range(2, half)]
-    order += [(1, 1), (half, 0)] + [(s, 1) for s in range(2, half + 1)]
+    order = [(s, h) for s in range(half + 1) for h in range(2)]
     stages = {0: stage_a, 2: stage_b, 4: stage_c, 6: stage_d}
 
     def give_all(n):

time: 108 us -> 106 us (0.981)
    pallas_call x1, Pallas kernels: 104 us -> 102 us  [per_device(): pl.pallas_call(functools.partial(kernel, dims), out_shape=(jax.ShapeDtype...]
where the time goes in v3:
time: 106 us
  Pallas kernels  105 us (99%)
  between operations  1.29 us (1%)
    pallas_call x1, Pallas kernels, per_device(): pl.pallas_call(functools.partial(kernel, dims), out_shape=(jax.ShapeDtype...  102 us
    pallas_call x1, Pallas kernels, per_device(): pl.pallas_call(write, out_shape=(jax.ShapeDtypeStruct((rows_dev, width),...  2.54 us

profile of v3, /device:TPU:0, one launch (start us, length us, event | category | flops | bytes accessed | tf_op | source)
XLA Modules:
  0.0 105.8 jit_solution(9559098902876447456)
XLA Ops:
  1.3 102.0 %graph_layer.1 = (bf16[384,512]{1,0:T(8,128)(2,1)}, bf16[384,512]{1,0:T(8,128)(2,1)}, bf16[4,128,512]{2,1,0:T(8,128)(2,1)}) custom-call(bf16[3,128,512]{2,1,0:T(8,128)(2,1)} %bitcast.8, bf16[512,512]{1,0:T(8,128)(2,1)} %weight.1, bf16[8,128,128]{2,1,0:T(8,128)(2,1)} %bitcast.9, s32[8]{0:T(128)} %bitcast.10, s32[8]{0:T(128)} %bitcast.11, ...), custom_call_target="tpu_custom_call" | custom-call | tf_op jit(solution)/shard_map/graph_layer/pallas_call | solution.py:422
  103.3 2.5 %write.1 = (bf16[384,512]{1,0:T(8,128)(2,1)}, bf16[384,512]{1,0:T(8,128)(2,1)}, f32[512,512]{1,0:T(8,128)}) custom-call(bf16[384,512]{1,0:T(8,128)(2,1)} %get-tuple-element.6.act, bf16[384,512]{1,0:T(8,128)(2,1)} %get-tuple-element.7.gf, bf16[512,512]{1,0:T(8,128)(2,1)} %bitcast.7), custom_call_target="tpu_custom_call" | custom-call | tf_op jit(solution)/shard_map/write/pallas_call | solution.py:474
